TPU v7x, 32 devices: a whole 2x2x4 slice. The times are simulated.
32 devices in a mesh: parts: 1, sec: 32 (over z, y, x, core).
Axes of the slice: x: 2, y: 2, z: 4, core: 2. Of those that a mesh axis runs over, the one named last changes fastest.
Arguments:
- queries: bfloat16 [8192, 1024], P(('parts', 'sec')), may hold values from -6 to 6
- keys: bfloat16 [8192, 1024], P(('parts', 'sec')), may hold values from -6 to 6
- values: bfloat16 [8192, 2048], P(('parts', 'sec')), may hold values from -6 to 6
- gate_codes: int32 [8192, 16], P(('parts', 'sec')), may hold values from 0 to 5734
- beta_codes: int32 [8192, 16], P(('parts', 'sec')), may hold values from 16 to 4096
- norm_gain: float32 [128], replicated, may hold values from 0.5 to 1.5
Outputs:
- head_out: bfloat16 [8192, 2048], P(('parts', 'sec'))
- final_state: float32 [2048, 128], P(('parts', 'sec'))
All inputs are finite; a program needn't handle non-finite values.
Results may differ from a plain program's by a relative error of at most 0.001.
Values sent between devices are 32-bit elements; how exact they have to be, the bound alone decides.
A program may use at most 320 MiB of HBM per device.

v0:
```python
import jax
import jax.numpy as jnp
from jax import lax
from jax.sharding import PartitionSpec as P

DK = 128
SPAN = 64


def entering(part, axis, combine, identity):
    place = lax.axis_index(axis)
    gathered = jax.tree.map(lambda a: lax.all_gather(a, axis), part)
    state = jax.tree.map(lambda a, e: jnp.zeros_like(a) + jnp.asarray(e, a.dtype), part, identity)

    def one(hop, state):
        return combine(
            state, jax.tree.map(lambda a: lax.dynamic_index_in_dim(a, hop, 0, False), gathered)
        )

    return lax.fori_loop(0, place, one, state)


def broadcast(value, axis, source):
    kept = jnp.where(lax.axis_index(axis) == source, value, 0).astype(value.dtype)
    return lax.psum(kept, axis)


def normalize(rows, factor):
    return rows * lax.rsqrt(jnp.sum(rows * rows, axis=-1, keepdims=True) + 1e-06) * factor


def matrix_product(form, left, right):
    return jnp.einsum(form, left, right, precision=lax.Precision.HIGHEST)


def compose(earlier, later):
    first_map, first_state = earlier
    second_map, second_state = later
    return (
        matrix_product("hij,hjk->hik", second_map, first_map),
        matrix_product("hij,hjv->hiv", second_map, first_state) + second_state,
    )


def block_step(carried, block_in):
    transition_matrix, state_matrix = carried
    query_rows, key_matrix, value_rows, log_decay, beta_rows = block_in
    length = query_rows.shape[1]
    key_width = key_matrix.shape[2]
    decay_factor = jnp.exp(jnp.cumsum(log_decay, axis=1))
    row_index = lax.broadcasted_iota(jnp.int32, (length, length), 0)
    col_ids = lax.broadcasted_iota(jnp.int32, (length, length), 1)
    strict_mask = (row_index > col_ids).astype(jnp.float32)
    lower_mask = (row_index >= col_ids).astype(jnp.float32)
    identity_c = jnp.eye(length, dtype=jnp.float32)
    inner_kk = matrix_product("hik,hjk->hij", key_matrix, key_matrix)
    coupling = beta_rows[:, :, None] * inner_kk * strict_mask
    inverse = identity_c - coupling
    power_mat = coupling
    for doubling in range(1, length.bit_length() - 1):
        power_mat = matrix_product("hij,hjk->hik", power_mat, power_mat)
        inverse = matrix_product("hij,hjk->hik", inverse, identity_c + power_mat)
    right_side = jnp.concatenate(
        [
            beta_rows[:, :, None] * key_matrix,
            beta_rows[:, :, None] * value_rows / decay_factor[:, :, None],
        ],
        axis=-1,
    )
    solved = matrix_product("hij,hjk->hik", inverse, right_side)
    erase_rows = solved[:, :, :key_width]
    written_rows = solved[:, :, key_width:]
    scores = matrix_product("hik,hjk->hij", query_rows, key_matrix) * lower_mask
    projected_value = decay_factor[:, :, None] * (
        query_rows - matrix_product("hij,hjk->hik", scores, erase_rows)
    )
    section_output = matrix_product("wjf,wft->wjt", projected_value, state_matrix) + decay_factor[
        :, :, None
    ] * matrix_product("hij,hjv->hiv", scores, written_rows)
    carried_transform = matrix_product("hik,hkm->him", projected_value, transition_matrix)
    final_decay = decay_factor[:, -1][:, None, None]
    erase_key = matrix_product("hjk,hjm->hkm", key_matrix, erase_rows)
    write_key = matrix_product("ius,iuc->isc", key_matrix, written_rows)
    transition_matrix = final_decay * (
        transition_matrix - matrix_product("hkm,hmn->hkn", erase_key, transition_matrix)
    )
    state_matrix = final_decay * (
        state_matrix - matrix_product("cjg,cgu->cju", erase_key, state_matrix) + write_key
    )
    return ((transition_matrix, state_matrix), (section_output, carried_transform))


def shards(queries, keys, values, gate_codes, beta_codes, norm_gain):
    tokens_dev, heads = gate_codes.shape
    width = norm_gain.shape[0]
    key_width = DK
    group = heads // (queries.shape[1] // key_width)
    sections = lax.axis_size("sec")
    total = tokens_dev * sections
    query_rows = normalize(
        queries.astype(jnp.float32).reshape(tokens_dev, -1, key_width), key_width ** (-0.5)
    )
    key_matrix = normalize(keys.astype(jnp.float32).reshape(tokens_dev, -1, key_width), 1.0)
    query_rows = jnp.repeat(query_rows, group, axis=1)
    key_matrix = jnp.repeat(key_matrix, group, axis=1)
    value_rows = values.astype(jnp.float32).reshape(tokens_dev, heads, width)
    log_decay = -gate_codes.astype(jnp.float32) / total
    beta_rows = beta_codes.astype(jnp.float32) / total
    count = tokens_dev // SPAN

    def blocked(array):
        shaped = array.reshape((count, SPAN) + array.shape[1:])
        return jnp.swapaxes(shaped, 1, 2)

    inputs = (
        blocked(query_rows),
        blocked(key_matrix),
        blocked(value_rows),
        blocked(log_decay),
        blocked(beta_rows),
    )
    identity_k = jnp.broadcast_to(
        jnp.eye(key_width, dtype=jnp.float32), (heads, key_width, key_width)
    )
    zero_state = jnp.zeros((heads, key_width, width), jnp.float32)
    (transition_matrix, state_matrix), (section_output, carried_transform) = lax.scan(
        block_step, (identity_k, zero_state), inputs
    )
    section_output = jnp.swapaxes(section_output, 0, 1).reshape(heads, tokens_dev, width)
    carried_transform = jnp.swapaxes(carried_transform, 0, 1).reshape(heads, tokens_dev, key_width)
    entering_state = entering(
        (transition_matrix, state_matrix), "sec", compose, (identity_k, zero_state)
    )[1]
    output_rows = section_output + matrix_product("wjf,wft->wjt", carried_transform, entering_state)
    scaled = (
        output_rows
        * lax.rsqrt(jnp.mean(output_rows * output_rows, axis=-1, keepdims=True) + 1e-06)
        * norm_gain
    )
    head_out = jnp.swapaxes(scaled, 0, 1).reshape(tokens_dev, heads * width).astype(jnp.bfloat16)
    ending_state = (
        matrix_product("cjg,cgu->cju", transition_matrix, entering_state) + state_matrix
    ).reshape(heads * key_width, width)
    row_count = heads * key_width // sections
    whole = broadcast(ending_state, "sec", sections - 1)
    final_state = lax.dynamic_slice_in_dim(whole, lax.axis_index("sec") * row_count, row_count, 0)
    return (head_out, final_state)


def solution(mesh):
    in_specs = (
        P(("parts", "sec"), None),
        P(("parts", "sec"), None),
        P(("parts", "sec"), None),
        P(("parts", "sec"), None),
        P(("parts", "sec"), None),
        P(),
    )
    out_specs = (P(("parts", "sec"), None), P(("parts", "sec"), None))
    return jax.shard_map(shards, mesh=mesh, in_specs=in_specs, out_specs=out_specs, check_vma=False)
```

profile of v0, /device:TPU:0, one launch (start us, length us, event | category | flops | bytes accessed | tf_op | source)
XLA Modules:
  0.0 778.5 jit_solution(4461835839426412052)
XLA Ops:
  8.1 1.1 convert_bitcast_fusion.2
  11.7 1.5 bitcast_bitcast_fusion
  15.5 1.5 broadcast_in_dim.17
  17.0 1.5 broadcast_in_dim.18
  18.6 139.3 %while.30 = (s32[]{:T(128)}, f32[16,128,128]{2,1,0:T(8,128)}, f32[16,128,128]{2,1,0:T(8,128)}, f32[4,16,64,128]{3,2,0,1:T(8,128)}, f32[4,16,64,128]{3,2,0,1:T(8,...) while((s32[]{:T(128)}, f32[16,128,128]{2,1,0:T(8,128)}, ...), condition=%wide.region_4.5_spmd.clone, body=%wide.region_2.4_spmd.clone.sunk | while | flops 2721602560 | bytes 44791276 | solution.py:126
  18.6 2.1 convolution_multiply_fusion.5
  20.8 2.2 fusion.206
  29.8 1.1 constant_dynamic-slice_fusion.7
  30.9 1.4 bitcast_multiply_fusion.2
  33.3 1.7 fusion.223
  35.0 1.4 copy.84
  36.4 2.0 fusion.225
  38.4 2.9 fusion.218
  41.5 2.2 fusion.219
  43.7 1.5 convolution_multiply_fusion.6
  45.2 3.1 fusion.224
  48.3 2.9 fusion.220
  51.2 2.3 fusion.221
  53.4 2.1 convolution_multiply_fusion.5
  55.6 2.2 fusion.206
  64.6 1.1 constant_dynamic-slice_fusion.7
  65.7 1.4 bitcast_multiply_fusion.2
  68.1 1.7 fusion.223
  69.9 1.4 copy.84
  71.3 1.9 fusion.225
  73.2 2.9 fusion.218
  76.3 2.2 fusion.219
  78.5 1.5 convolution_multiply_fusion.6
  80.0 3.1 fusion.224
  83.1 2.9 fusion.220
  86.0 2.3 fusion.221
  88.2 2.1 convolution_multiply_fusion.5
  90.4 2.2 fusion.206
  100.5 1.4 bitcast_multiply_fusion.2
  102.9 1.7 fusion.223
  104.7 1.4 copy.84
  106.1 1.9 fusion.225
  108.0 2.9 fusion.218
  111.1 2.2 fusion.219
  113.3 1.5 convolution_multiply_fusion.6
  114.9 3.1 fusion.224
  117.9 2.9 fusion.220
  120.8 2.3 fusion.221
  123.1 2.1 convolution_multiply_fusion.5
  125.3 2.2 fusion.206
  135.4 1.4 bitcast_multiply_fusion.2
  137.8 1.7 fusion.223
  139.5 1.4 copy.84
  140.9 1.9 fusion.225
  142.9 2.9 fusion.218
  145.9 2.2 fusion.219
  148.1 1.5 convolution_multiply_fusion.6
  149.7 3.1 fusion.224
  152.8 2.9 fusion.220
  155.7 2.3 fusion.221
  159.5 1.8 copy.33
  161.3 194.2 %all-gather.5.cloned.1.call-done = f32[512,128,128]{2,1,0:T(8,128)} async-done(((f32[16,128,128]{2,1,0:T(8,128)}), f32[512,128,128]{2,1,0:T(8,128)}) %all-gather.5.cloned.1.call-update) | async-done | bytes 33554448 | tf_op jit(solution)/shard_map/all_gather | solution.py:12
  355.6 195.8 %all-gather.7.cloned.1.call-done = f32[512,128,128]{2,1,0:T(8,128)} async-done(((f32[16,128,128]{2,1,0:T(8,128)}), f32[512,128,128]{2,1,0:T(8,128)}) %all-gather.7.cloned.1.call-update) | async-done | bytes 33554448 | tf_op jit(solution)/shard_map/all_gather | solution.py:12
  551.5 1.2 copy-done.2
  552.7 3.4 fusion.62
  556.2 4.4 multiply_reduce_fusion
  561.2 1.4 copy.34
  562.6 208.0 %all-reduce.2.cloned.1.call-done = f32[2048,128]{1,0:T(8,128)} async-done(((f32[2048,128]{1,0:T(8,128)}), f32[2048,128]{1,0:T(8,128)}) %all-reduce.2.cloned.1.call-update) | async-done | bytes 1048592 | tf_op jit(solution)/shard_map/psum | solution.py:25
  770.6 1.4 constant_dynamic-slice_fusion.3
  (137 shorter events, 42.1 us)
Async XLA Ops:
  7.2 348.4 %all-gather.5.cloned.1.call-start = ((), (), s32[]{:S(2)}) async-start(), calls=%async_computation.1 | async-start | bytes 34603008 | tf_op jit(solution)/shard_map/all_gather | solution.py:12
  9.8 0.7 copy-start.6
  9.8 1.2 copy-start.4
  11.7 1.5 copy-start.5
  35.0 3.4 copy-start
  41.5 3.7 copy-start.1
  69.9 3.3 copy-start
  76.2 3.7 copy-start.1
  104.7 3.4 copy-start
  111.1 3.7 copy-start.1
  139.5 3.4 copy-start
  145.9 3.7 copy-start.1
  157.9 1.6 copy-start.3
  157.9 393.5 %all-gather.7.cloned.1.call-start = ((), (), s32[]{:S(2)}) async-start(), calls=%async_computation.2 | async-start | bytes 34603008 | tf_op jit(solution)/shard_map/all_gather | solution.py:12
  158.7 611.9 %all-reduce.2.cloned.1.call-start = ((), (), s32[]{:S(2)}) async-start(), calls=%async_computation | async-start | bytes 2097152 | tf_op jit(solution)/shard_map/psum | solution.py:25
  551.5 1.2 copy-start.2
  556.2 4.4 copy-start.7
Sparse Core Ops, SparseCore 0:
  158.1 197.4 all-gather.4
  358.4 192.9 all-gather.6
  556.6 213.9 all-reduce.1
where the time goes:
time: 781 us; the launch traced here: 778 us
  waiting for transfers between devices  599 us (77%)
  matrix products  129 us (17%)
  local copies, waits for them, and re-layouts  25.4 us (3%)
  between operations  14 us (2%)
  other arithmetic  10.7 us (1%)
    all_gather x2, waiting for transfers between devices, entering(): gathered = jax.tree.map(lambda a: lax.all_gather(a, axis), part)  390 us
    psum x1, waiting for transfers between devices, broadcast(): return lax.psum(kept, axis)  208 us
    dot_general x86, matrix products, matrix_product(): return jnp.einsum(form, left, right, precision=lax.Precision.HIGHEST)  129 us
  transfers between devices with their start and end apart: 3, of which 3 were waited for; matrix products, arithmetic and copies ran while one was open for 1% of the time, Pallas kernels for 0%

commit v1 on v0

--- a/solution.py
+++ b/solution.py
@@ -22,7 +22,7 @@
 
 def broadcast(value, axis, source):
     kept = jnp.where(lax.axis_index(axis) == source, value, 0).astype(value.dtype)
-    return lax.psum(kept, axis)
+    return jnp.sum(lax.all_gather(kept, axis), axis=0)
 
 
 def normalize(rows, factor):

time: 781 us -> 857 us (1.097)
  waiting for transfers between devices: 599 us -> 663 us
  other arithmetic: 10.7 us -> 22.4 us
    all_gather x0 -> x1, waiting for transfers between devices: none -> 270 us  [broadcast(): return jnp.sum(lax.all_gather(kept, axis), axis=0)]
    psum x1 -> x0, waiting for transfers between devices: 208 us -> none  [broadcast(): return lax.psum(kept, axis)]
    reduce_sum x0 -> x1, other arithmetic: none -> 11.7 us  [broadcast(): return jnp.sum(lax.all_gather(kept, axis), axis=0)]
where the time goes in v1:
time: 857 us; the launch traced here: 854 us
  waiting for transfers between devices  663 us (77%)
  matrix products  128 us (15%)
  local copies, waits for them, and re-layouts  25 us (3%)
  other arithmetic  22.4 us (3%)
  between operations  14 us (2%)
    all_gather x2, waiting for transfers between devices, entering(): gathered = jax.tree.map(lambda a: lax.all_gather(a, axis), part)  393 us
    all_gather x1, waiting for transfers between devices, broadcast(): return jnp.sum(lax.all_gather(kept, axis), axis=0)  270 us
    dot_general x86, matrix products, matrix_product(): return jnp.einsum(form, left, right, precision=lax.Precision.HIGHEST)  128 us
  transfers between devices with their start and end apart: 3, of which 3 were waited for; matrix products, arithmetic and copies ran while one was open for 1% of the time, Pallas kernels for 0%

profile of v1, /device:TPU:0, one launch (start us, length us, event | category | flops | bytes accessed | tf_op | source)
XLA Modules:
  0.0 854.0 jit_solution(3440577896672549136)
XLA Ops:
  8.1 1.1 convert_bitcast_fusion.2
  11.7 1.5 bitcast_bitcast_fusion
  15.5 1.5 broadcast_in_dim.17
  17.0 1.5 broadcast_in_dim.18
  18.6 139.0 %while.30 = (s32[]{:T(128)}, f32[16,128,128]{2,1,0:T(8,128)}, f32[16,128,128]{2,1,0:T(8,128)}, f32[4,16,64,128]{3,2,0,1:T(8,128)}, f32[4,16,64,128]{3,2,0,1:T(8,...) while((s32[]{:T(128)}, f32[16,128,128]{2,1,0:T(8,128)}, ...), condition=%wide.region_4.5_spmd.clone, body=%wide.region_2.4_spmd.clone.sunk | while | flops 2721602560 | bytes 44791276 | solution.py:126
  18.6 2.1 convolution_multiply_fusion.5
  20.8 2.2 fusion.206
  30.8 1.4 bitcast_multiply_fusion.2
  33.3 1.7 fusion.223
  35.0 1.4 copy.84
  36.4 1.9 fusion.225
  38.3 2.9 fusion.218
  41.4 2.2 fusion.219
  43.6 1.5 convolution_multiply_fusion.6
  45.2 3.0 fusion.224
  48.2 2.9 fusion.220
  51.1 2.3 fusion.221
  53.3 2.1 convolution_multiply_fusion.5
  55.5 2.2 fusion.206
  64.5 1.1 constant_dynamic-slice_fusion.7
  65.6 1.4 bitcast_multiply_fusion.2
  68.0 1.7 fusion.223
  69.8 1.4 copy.84
  71.2 1.9 fusion.225
  73.1 2.9 fusion.218
  76.1 2.2 fusion.219
  78.4 1.5 convolution_multiply_fusion.6
  79.9 3.1 fusion.224
  83.0 2.9 fusion.220
  85.8 2.3 fusion.221
  88.1 2.1 convolution_multiply_fusion.5
  90.3 2.2 fusion.206
  99.3 1.1 constant_dynamic-slice_fusion.7
  100.4 1.4 bitcast_multiply_fusion.2
  102.8 1.7 fusion.223
  104.5 1.4 copy.84
  105.9 1.9 fusion.225
  107.8 2.9 fusion.218
  110.9 2.2 fusion.219
  113.1 1.5 convolution_multiply_fusion.6
  114.7 3.0 fusion.224
  117.7 2.9 fusion.220
  120.6 2.3 fusion.221
  122.8 2.1 convolution_multiply_fusion.5
  125.0 2.2 fusion.206
  135.1 1.4 bitcast_multiply_fusion.2
  137.5 1.7 fusion.223
  139.3 1.4 copy.84
  140.7 1.9 fusion.225
  142.6 2.9 fusion.218
  145.6 2.2 fusion.219
  147.9 1.5 convolution_multiply_fusion.6
  149.4 3.1 fusion.224
  152.5 2.9 fusion.220
  155.3 2.3 fusion.221
  158.4 196.8 %all-gather.8.cloned.1.call-done = f32[512,128,128]{2,1,0:T(8,128)} async-done(((f32[16,128,128]{2,1,0:T(8,128)}), f32[512,128,128]{2,1,0:T(8,128)}) %all-gather.8.cloned.1.call-update) | async-done | bytes 33554448 | tf_op jit(solution)/shard_map/all_gather | solution.py:12
  355.3 195.8 %all-gather.10.cloned.1.call-done = f32[512,128,128]{2,1,0:T(8,128)} async-done(((f32[16,128,128]{2,1,0:T(8,128)}), f32[512,128,128]{2,1,0:T(8,128)}) %all-gather.10.cloned.1.call-update) | async-done | bytes 33554448 | tf_op jit(solution)/shard_map/all_gather | solution.py:12
  551.2 1.2 copy-done.2
  552.4 3.4 fusion.62
  555.8 2.9 copy.33
  558.7 4.4 multiply_reduce_fusion
  563.7 1.4 copy.34
  565.2 270.0 %all-gather.6.cloned.1.call-done = f32[32,2048,128]{2,1,0:T(8,128)} async-done(((f32[1,2048,128]{2,1,0:T(8,128)}), f32[32,2048,128]{2,1,0:T(8,128)}) %all-gather.6.cloned.1.call-update) | async-done | bytes 33554448 | tf_op jit(solution)/shard_map/all_gather | solution.py:25
  835.1 11.7 %reduce_sum.39 = f32[2048,128]{1,0:T(8,128)S(1)} reduce(f32[32,2048,128]{2,1,0:T(8,128)} %all-gather.6.cloned.1.call-done, f32[]{:T(128)} %constant.52.clone.1), dimensions={0}, to_apply=%region_8.9 | reduce | flops 8126464 | bytes 34603012 | tf_op jit(solution)/shard_map/reduce_sum | solution.py:25
  (136 shorter events, 41.9 us)
Async XLA Ops:
  7.2 348.1 %all-gather.8.cloned.1.call-start = ((), (), s32[]{:S(2)}) async-start(), calls=%async_computation.1 | async-start | bytes 34603008 | tf_op jit(solution)/shard_map/all_gather | solution.py:12
  9.8 0.7 copy-start.5
  9.8 1.2 copy-start.3
  11.7 1.5 copy-start.4
  35.0 3.4 copy-start
  41.4 3.7 copy-start.1
  69.7 3.3 copy-start
  76.1 3.7 copy-start.1
  104.5 3.3 copy-start
  110.9 3.7 copy-start.1
  139.2 3.3 copy-start
  145.6 3.7 copy-start.1
  157.6 393.5 %all-gather.10.cloned.1.call-start = ((), (), s32[]{:S(2)}) async-start(), calls=%async_computation.2 | async-start | bytes 34603008 | tf_op jit(solution)/shard_map/all_gather | solution.py:12
  158.4 676.8 %all-gather.6.cloned.1.call-start = ((), (), s32[]{:S(2)}) async-start(), calls=%async_computation | async-start | bytes 34603008 | tf_op jit(solution)/shard_map/all_gather | solution.py:25
  551.2 1.2 copy-start.2
  558.7 4.4 copy-start.6
Sparse Core Ops, SparseCore 0:
  157.7 197.4 all-gather.7
  358.1 192.9 all-gather.9
  555.9 279.1 all-gather.5
